TPU v7x, 512 devices: a whole 4x4x16 slice. The times are simulated.
512 devices in a mesh: gx: 8 (over y, core), gy: 16 (over z), gz: 4 (over x).
Axes of the slice: x: 4, y: 4, z: 16, core: 2. Of those that a mesh axis runs over, the one named last changes fastest.
Arguments:
- cotangent: float32 [3, 32, 512, 1024], P(None, 'gz', 'gy', 'gx'), may hold values from -9 to 9
- closure: int32 [2, 1024, 32], P(None, 'gx', 'gz'), may hold values from 0 to 2
- owner: int32 [1024, 512], P('gx', 'gy'), may hold values from 0 to 511, as said below
- blowing: float32 [3], replicated, may hold values from 0.5 to 2
Outputs:
- gradient: float32 [3, 32, 512, 1024], P(None, 'gz', 'gy', 'gx')
- actuator_grad: float32 [512], P(('gx', 'gy', 'gz'))
Inputs may be any that keep to these rules, and one draw needn't show every extreme that they name: `owner`: the wall is cut into blocks of 32 x 32 cells aligned to multiples of those sizes; each block belongs to one actuator and each actuator owns exactly one block.
All inputs are finite; a program needn't handle non-finite values.
Results may differ from a plain program's by a relative error of at most 0.0009.
Values sent between devices are 32-bit elements; how exact they have to be, the bound alone decides.
A program may use at most 64 MiB of HBM per device.

v0:
```python
from functools import reduce

import jax
import jax.numpy as jnp
from jax import lax
from jax.sharding import PartitionSpec as P

deriv_alpha = 1.0 / 3.0
deriv_near = 14.0 / 9.0
deriv_far = 1.0 / 9.0
filter_alpha = 0.499
filter_coefs = [
    (193.0 + 126.0 * filter_alpha) / 256.0,
    (105.0 + 302.0 * filter_alpha) / 256.0,
    15.0 * (2.0 * filter_alpha - 1.0) / 64.0,
    45.0 * (1.0 - 2.0 * filter_alpha) / 512.0,
    5.0 * (2.0 * filter_alpha - 1.0) / 256.0,
    (1.0 - 2.0 * filter_alpha) / 512.0,
]


def prefix_2(value, axis, combine, identity, reverse):
    count, here = (lax.axis_size(axis), lax.axis_index(axis))
    everything = lax.all_gather(value, axis)
    start = jnp.broadcast_to(jnp.asarray(identity, value.dtype), value.shape)

    def hop(k, before):
        at = count - 1 - k if reverse else k
        reached = at > here if reverse else at < here
        new = combine(before, everything[at])
        return jnp.where(reached, new, before)

    return lax.fori_loop(0, count, hop, start)


def padded_2(cells, sides, width):
    for axis, dim in sides:
        count = lax.axis_size(axis)
        ends = count - 1
        head = lax.slice_in_dim(cells, 0, width, axis=dim)
        tail = lax.slice_in_dim(cells, cells.shape[dim] - width, cells.shape[dim], axis=dim)
        cells = jnp.concatenate(
            [
                lax.ppermute(tail, axis, [(i, (i + 1) % count) for i in range(ends)]),
                cells,
                lax.ppermute(head, axis, [((i + 1) % count, i) for i in range(ends)]),
            ],
            axis=dim,
        )
    return cells


def rescaled(entries):
    largest = reduce(jnp.maximum, [jnp.abs(entry) for entry in entries])
    return [entry / largest for entry in entries]


def matrix_product(later_map, earlier_map):
    result = []
    for row_index in range(3):
        for col_index in range(3):
            result.append(
                later_map[3 * row_index] * earlier_map[col_index]
                + later_map[3 * row_index + 1] * earlier_map[3 + col_index]
                + later_map[3 * row_index + 2] * earlier_map[6 + col_index]
            )
    return result


def combine_forward(earlier_map, later_map):
    product = matrix_product(
        [later_map[entry_index] for entry_index in range(9)],
        [earlier_map[entry_index] for entry_index in range(9)],
    )
    return jnp.stack(rescaled(product))


def combine_backward(earlier_map, later_map):
    return jnp.stack([later_map[0] * earlier_map[0], later_map[0] * earlier_map[1] + later_map[1]])


def forward_identity(sample):
    all_ones = jnp.ones_like(sample[0])
    nought = jnp.zeros_like(all_ones)
    return jnp.stack([all_ones, nought, nought, nought, all_ones, nought, nought, nought, all_ones])


def backward_identity(sample):
    return jnp.stack([jnp.ones_like(sample[0]), jnp.zeros_like(sample[0])])


def forward_composite(line_rows, lower_of, upper_of):
    all_ones = jnp.ones_like(line_rows[0])
    nought = jnp.zeros_like(all_ones)
    entries = [all_ones, nought, nought, nought, all_ones, nought, nought, nought, all_ones]
    for row_index, values in enumerate(line_rows):
        below_coef = lower_of(row_index)
        above_coef = upper_of(row_index)
        entries = [
            above_coef * entries[6],
            above_coef * entries[7],
            above_coef * entries[8],
            values * entries[6] - below_coef * entries[3],
            values * entries[7] - below_coef * entries[4],
            values * entries[8] - below_coef * entries[5],
            entries[6] - below_coef * entries[0],
            entries[7] - below_coef * entries[1],
            entries[8] - below_coef * entries[2],
        ]
        if row_index % 8 == 7:
            entries = rescaled(entries)
    return jnp.stack(rescaled(entries))


def solve_line(line_rows, lower_of, upper_of, forward_link, backward_link):
    composite = forward_composite(line_rows, lower_of, upper_of)
    carry_state = forward_link(composite)
    carry_c = carry_state[0] / carry_state[2]
    carry_d = carry_state[1] / carry_state[2]
    primes_c = []
    primes_d = []
    for row_index, values in enumerate(line_rows):
        below_coef = lower_of(row_index)
        pivot_value = 1.0 - below_coef * carry_c
        carry_c = upper_of(row_index) / pivot_value
        carry_d = (values - below_coef * carry_d) / pivot_value
        primes_c.append(carry_c)
        primes_d.append(carry_d)
    slope_term = jnp.ones_like(line_rows[0])
    offset = jnp.zeros_like(line_rows[0])
    for row_index in reversed(range(len(line_rows))):
        slope_term = -primes_c[row_index] * slope_term
        offset = primes_d[row_index] - primes_c[row_index] * offset
    following = backward_link(jnp.stack([slope_term, offset]))
    solution = [None] * len(line_rows)
    for row_index in reversed(range(len(line_rows))):
        following = primes_d[row_index] - primes_c[row_index] * following
        solution[row_index] = following
    return jnp.stack(solution, axis=0)


def forward_y(composite):
    prefix = prefix_2(composite, "gy", combine_forward, forward_identity(composite), False)
    return (prefix[2], prefix[5], prefix[8])


def backward_y(affine_pair):
    prefix = prefix_2(affine_pair, "gy", combine_backward, backward_identity(affine_pair), True)
    return prefix[1]


def forward_x(composite):
    prefix = prefix_2(composite, "gx", combine_forward, forward_identity(composite), False)
    return (prefix[2], prefix[5], prefix[8])


def backward_x(affine_pair):
    prefix = prefix_2(affine_pair, "gx", combine_backward, backward_identity(affine_pair), True)
    return prefix[1]


def filter_rows(solved, padded):
    length_first = solved.shape[0]
    filtered = filter_coefs[0] * solved
    for reach_cells in range(1, 6):
        filtered = filtered + 0.5 * filter_coefs[reach_cells] * (
            padded[5 + reach_cells : 5 + reach_cells + length_first]
            + padded[5 - reach_cells : 5 - reach_cells + length_first]
        )
    return filtered


def derive_rows(potential, rimmed):
    length_first = potential.shape[0]
    return -(
        0.5 * deriv_near * (rimmed[3 : 3 + length_first] - rimmed[1 : 1 + length_first])
        + 0.25 * deriv_far * (rimmed[4 : 4 + length_first] - rimmed[0:length_first])
    )


def on_device(cotangent, closure, owner, blowing):
    fields, width_z, width_y, width_x = cotangent.shape
    coupling = jnp.transpose(0.5 * filter_alpha * closure.astype(jnp.float32), (0, 2, 1))
    line_y = width_y * lax.axis_size("gy")
    start_y = lax.axis_index("gy") * width_y
    batch_y = fields * width_z * width_x
    rows_y = jnp.transpose(cotangent, (2, 0, 1, 3)).reshape(width_y, batch_y)
    couple_rows = jnp.broadcast_to(coupling[:, None], (2, fields, width_z, width_x)).reshape(
        2, batch_y
    )

    def lower_y(row_index):
        return jnp.where(start_y + row_index == 1, couple_rows[0], filter_alpha)

    def upper_y(row_index):
        return jnp.where(start_y + row_index == line_y - 2, couple_rows[1], filter_alpha)

    solved = solve_line(
        [rows_y[row_index] for row_index in range(width_y)], lower_y, upper_y, forward_y, backward_y
    )
    padded = padded_2(solved, (("gy", 0),), 5)
    filtered = filter_rows(solved, padded)
    rows_x = jnp.transpose(
        filtered.reshape(width_y, fields, width_z, width_x), (3, 1, 2, 0)
    ).reshape(width_x, fields * width_z * width_y)

    def constant_x(row_index):
        return deriv_alpha

    potential = solve_line(
        [rows_x[row_index] for row_index in range(width_x)],
        constant_x,
        constant_x,
        forward_x,
        backward_x,
    )
    rimmed = padded_2(potential, (("gx", 0),), 2)
    derivative = derive_rows(potential, rimmed)
    gradient = jnp.transpose(derivative.reshape(width_x, fields, width_z, width_y), (1, 2, 3, 0))
    surface = jnp.sum(blowing[:, None, None] * gradient[:, 0, :, :], axis=0)
    actuator_count = lax.axis_size("gx") * lax.axis_size("gy") * lax.axis_size("gz")
    patch_count = lax.axis_size("gz")
    patch_width = width_x // patch_count
    patch_sums = jnp.sum(surface.reshape(width_y, patch_count, patch_width), axis=(0, 2))
    patch_owner = owner[0::patch_width, 0]
    labels = lax.broadcasted_iota(jnp.int32, (1, actuator_count), 1)
    onehot = (patch_owner[:, None] == labels).astype(jnp.float32)
    wall_term = jnp.sum(patch_sums[:, None] * onehot, axis=0)
    wall_term = jnp.where(lax.axis_index("gz") == 0, wall_term, 0.0)
    actuator_grad = lax.psum_scatter(wall_term, ("gx", "gy", "gz"), scatter_dimension=0, tiled=True)
    return (gradient, actuator_grad)


def solution(mesh):
    in_specs = (P(None, "gz", "gy", "gx"), P(None, "gx", "gz"), P("gx", "gy"), P())
    out_specs = (P(None, "gz", "gy", "gx"), P(("gx", "gy", "gz")))
    return jax.shard_map(
        on_device, mesh=mesh, in_specs=in_specs, out_specs=out_specs, check_vma=False
    )
```

profile of v0, /device:TPU:1, one launch (start us, length us, event | category | flops | bytes accessed | tf_op | source)
XLA Modules:
  0.0 363.8 jit_solution(13164988881768872552)
XLA Ops:
  7.3 1.9 fusion.396
  9.2 2.3 fusion.395
  11.6 0.7 multiply_bitcast_fusion
  13.0 0.6 multiply_subtract_fusion.139
  13.8 0.6 multiply_subtract_fusion.112
  14.8 0.6 multiply_subtract_fusion.88
  15.7 0.6 fusion.385
  16.3 1.4 stack.587
  17.8 73.1 %all-gather.10.cloned.1.call-done = f32[16,9,3072]{2,1,0:T(8,128)} async-done(((f32[1,9,3072]{2,1,0:T(8,128)}), f32[16,9,3072]{2,1,0:T(8,128)}) %all-gather.10.cloned.1.call-update) | async-done | bytes 1769488 | tf_op jit(solution)/shard_map/all_gather | solution.py:24
  90.8 34.5 %while.56 = (s32[]{:T(128)}, f32[9,3072]{1,0:T(8,128)S(1)}, s32[]{:T(128)}, f32[16,9,3072]{2,1,0:T(8,128)}, s32[]{:T(128)}, /*index=5*/s32[]{:T(128)}, s32[]{}, ...) while((s32[]{:T(128)}, f32[9,3072]{1,0:T(8,128)S(1)}, s32[]{:T(128)}, f32[16,9,3072]{2,1,0:T(8,128)}, ...), condition=%wide.region_1.2_spmd, body=%wide.region_0.1_spmd.sunk | while | flops 245771 | bytes 1106195 | solution.py:33
  90.8 1.8 fusion.402
  93.0 1.9 fusion.402
  95.2 1.8 fusion.402
  97.3 1.8 fusion.402
  99.5 1.8 fusion.402
  101.6 1.8 fusion.402
  103.8 1.8 fusion.402
  105.9 1.6 fusion.402
  107.9 1.8 fusion.402
  110.1 1.9 fusion.402
  112.3 2.0 fusion.402
  114.6 1.8 fusion.402
  116.7 1.8 fusion.402
  118.9 1.9 fusion.402
  121.1 1.8 fusion.402
  123.2 1.8 fusion.402
  125.4 1.0 multiply_multiply_fusion
  126.4 1.7 multiply_subtract_fusion.32
  128.1 22.5 %all-gather.5 = f32[16,2,3072]{2,1,0:T(2,128)S(1)} all-gather(f32[1,2,3072]{2,1,0:T(2,128)S(1)} %maximum_bitcast_fusion), channel_id=3, replica_groups=mesh['gx'=8,'gy'=16,'gz'=4] {'gy'}, dimensions={0}, use_global_device_ids=true | all-gather | bytes 417792 | tf_op jit(solution)/shard_map/all_gather | solution.py:24
  150.6 1.8 while.57
  152.4 0.7 multiply_subtract_fusion
  153.2 1.3 collective-permute-start
  154.6 4.2 %collective-permute-start.1 = (f32[5,3072]{1,0:T(8,128)S(1)}, f32[5,3072]{1,0:T(8,128)S(1)}, u32[]{:S(2)}, u32[]{:S(2)}) collective-permute-start(f32[5,3072]{1,0:T(8,128)S(1)} %stack.591), channel_id=1, source_target_pairs={{0,4},{4,8},{8,12},{12,16},{16,20},{20,24},{24,28},{28,32},{32,36}... | collective-permute-start | bytes 184328 | tf_op jit(solution)/shard_map/ppermute | solution.py:44
  158.8 0.8 slice.1399
  159.6 3.1 stack.589
  162.7 3.0 concatenate.59
  165.7 0.7 concatenate.51
  166.5 3.1 concatenate.60
  169.5 0.6 concatenate.52
  170.1 0.7 concatenate.53
  170.9 0.6 concatenate.54
  171.5 4.7 %concatenate.55 = f32[34,3072]{1,0:T(8,128)} concatenate(f32[1,3072]{1,0:T(1,128)S(1)} %get-tuple-element.793, f32[1,3072]{1,0:T(1,128)S(1)} %get-tuple-element.794, f32[1,3072]{1,0:T(1,128)S(1)} %get-tuple-element.795, f32[1,3072]{1,0:T(1,128)S(1)} %get-tuple-element.796, f32[1,3072]{1,0:T(1,128)S(1)} %get-tuple-element.797, f32[1,3072]{1,0:T(1,128)S(1)} %get-tuple-element.798, ...), dimensions={0} | concatenate | bytes 835584 | tf_op jit(solution)/shard_map/concatenate | solution.py:42
  176.2 3.7 %concatenate.56 = f32[34,3072]{1,0:T(8,128)} concatenate(f32[5,3072]{1,0:T(8,128)S(1)} %collective-permute-done.1, f32[1,3072]{1,0:T(1,128)S(1)} %get-tuple-element.790, f32[1,3072]{1,0:T(1,128)S(1)} %get-tuple-element.791, f32[1,3072]{1,0:T(1,128)S(1)} %get-tuple-element.792, f32[1,3072]{1,0:T(1,128)S(1)} %get-tuple-element.793, f32[1,3072]{1,0:T(1,128)S(1)} %get-tuple-element.794, ...), dimensions={0} | concatenate | bytes 835584 | tf_op jit(solution)/shard_map/concatenate | solution.py:42
  179.9 0.7 concatenate.57
  180.6 0.5 concatenate.58
  181.1 1.9 fusion.8
  183.1 0.6 copy.12
  194.2 31.4 %all-gather.6 = f32[8,9,768]{2,1,0:T(8,128)S(1)} all-gather(f32[1,9,768]{2,1,0:T(8,128)S(1)} %bitcast.968), channel_id=4, replica_groups=mesh['gx'=8,'gy'=16,'gz'=4] {'gx'}, dimensions={0}, use_global_device_ids=true | all-gather | bytes 248832 | tf_op jit(solution)/shard_map/all_gather | solution.py:24
  225.7 1.8 while.58
  227.5 1.1 multiply_multiply_fusion.2
  228.6 0.8 multiply_subtract_fusion.297
  229.5 13.0 %all-gather.7 = f32[8,2,768]{2,1,0:T(2,128)S(1)} all-gather(f32[1,2,768]{2,1,0:T(2,128)S(1)} %maximum_bitcast_fusion.1), channel_id=5, replica_groups=mesh['gx'=8,'gy'=16,'gz'=4] {'gx'}, dimensions={0}, use_global_device_ids=true | all-gather | bytes 55296 | tf_op jit(solution)/shard_map/all_gather | solution.py:24
  242.5 0.5 while.59
  243.1 0.5 multiply_subtract_fusion.169
  243.7 2.9 collective-permute-start.3
  247.3 1.9 collective-permute-start.2
  250.0 2.3 collective-permute-done.2
  252.3 0.8 concatenate.63
  253.1 0.9 concatenate.61
  254.0 0.8 concatenate.64
  254.8 0.8 concatenate.62
  255.9 0.3 copy-done.5
  256.7 99.7 %all-reduce = f32[512]{0:T(512)S(1)} all-reduce(f32[512]{0:T(512)S(1)} %broadcast_select_fusion.2), channel_id=6, replica_groups=mesh['gx'=8,'gy'=16,'gz'=4] {'gx','gy','gz'}, use_global_device_ids=true, to_apply=%region_11.12.clone | all-reduce | flops 512 | bytes 4096
  356.4 0.6 dynamic-slice
  (530 shorter events, 20.8 us)
Async XLA Ops:
  7.2 83.7 %all-gather.10.cloned.1.call-start = ((), (), s32[]{:S(2)}) async-start(), calls=%async_computation | async-start | bytes 3342336 | tf_op jit(solution)/shard_map/all_gather | solution.py:24
  14.7 76.1 %copy-start = (f32[9,3072]{1,0:T(8,128)S(1)}, f32[9,3072]{1,0:T(8,128)}, u32[]{:S(2)}) copy-start(f32[9,3072]{1,0:T(8,128)} %constant.533.clone.1) | copy-start | bytes 331780
  125.4 25.3 %copy-start.2 = (f32[2,3072]{1,0:T(2,128)S(1)}, f32[2,3072]{1,0:T(2,128)}, u32[]{:S(2)}) copy-start(f32[2,3072]{1,0:T(2,128)} %constant.567.clone.1) | copy-start | bytes 73732
  153.2 9.5 %collective-permute-start = (f32[5,3072]{1,0:T(8,128)S(1)}, f32[5,3072]{1,0:T(8,128)S(1)}, u32[]{:S(2)}, u32[]{:S(2)}) collective-permute-start(f32[5,3072]{1,0:T(8,128)S(1)} %stack.590), channel_id=1, source_target_pairs={{4,0},{8,4},{12,8},{16,12},{20,16},{24,20},{28,24},{32,28},{36,32}... | collective-permute-start | bytes 184328 | tf_op jit(solution)/shard_map/ppermute | solution.py:46
  154.6 11.9 %collective-permute-start.1 = (f32[5,3072]{1,0:T(8,128)S(1)}, f32[5,3072]{1,0:T(8,128)S(1)}, u32[]{:S(2)}, u32[]{:S(2)}) collective-permute-start(f32[5,3072]{1,0:T(8,128)S(1)} %stack.591), channel_id=1, source_target_pairs={{0,4},{4,8},{8,12},{12,16},{16,20},{20,24},{24,28},{28,32},{32,36}... | collective-permute-start | bytes 184328 | tf_op jit(solution)/shard_map/ppermute | solution.py:44
  191.2 34.5 %copy-start.1 = (f32[9,768]{1,0:T(8,128)S(1)}, f32[9,768]{1,0:T(8,128)}, u32[]{:S(2)}) copy-start(f32[9,768]{1,0:T(8,128)} %constant.574.clone.1) | copy-start | bytes 82948
  225.7 16.8 %copy-start.3 = (f32[2,768]{1,0:T(2,128)S(1)}, f32[2,768]{1,0:T(2,128)}, u32[]{:S(2)}) copy-start(f32[2,768]{1,0:T(2,128)} %constant.595.clone.1) | copy-start | bytes 18436
  243.7 10.3 %collective-permute-start.3 = (f32[2,768]{1,0:T(2,128)S(1)}, f32[2,768]{1,0:T(2,128)S(1)}, u32[]{:S(2)}, u32[]{:S(2)}) collective-permute-start(f32[2,768]{1,0:T(2,128)S(1)} %pad_maximum_fusion.1), channel_id=1, source_target_pairs={{0,64},{64,128},{128,192},{192,256},{256,320},{320,384},{384,448},... | collective-permute-start | bytes 18440 | tf_op jit(solution)/shard_map/ppermute | solution.py:44
  247.3 4.9 %collective-permute-start.2 = (f32[2,768]{1,0:T(2,128)S(1)}, f32[2,768]{1,0:T(2,128)S(1)}, u32[]{:S(2)}, u32[]{:S(2)}) collective-permute-start(f32[2,768]{1,0:T(2,128)S(1)} %pad_maximum_fusion), channel_id=1, source_target_pairs={{64,0},{128,64},{192,128},{256,192},{320,256},{384,320},{448,384},... | collective-permute-start | bytes 18440 | tf_op jit(solution)/shard_map/ppermute | solution.py:46
  255.6 0.7 copy-start.5
  255.9 101.0 %copy-start.4 = (f32[128,768]{0,1:T(8,128)}, f32[128,768]{0,1:T(8,128)S(1)}, u32[]{:S(2)}) copy-start(f32[128,768]{0,1:T(8,128)S(1)} %copy.13) | copy-start | bytes 1179652
Sparse Core Ops, SparseCore 0:
  17.9 72.8 all-gather.9
where the time goes:
time: 365 us; the launch traced here: 364 us
  blocking collectives  167 us (46%)
  waiting for transfers between devices  75.3 us (21%)
  local copies, waits for them, and re-layouts  46.8 us (13%)
  other arithmetic  46.7 us (13%)
  between operations  16.4 us (4%)
  starting transfers between devices  10.3 us (3%)
    unnamed x1, blocking collectives  99.7 us
    all_gather x1, waiting for transfers between devices, prefix_2(): everything = lax.all_gather(value, axis)  73.1 us
    all_gather x3, blocking collectives, prefix_2(): everything = lax.all_gather(value, axis)  67 us
    div x52, other arithmetic, rescaled(): return [entry / largest for entry in entries]  32 us
    concatenate x14, local copies, waits for them, and re-layouts, padded_2(): jnp.concatenate([lax.ppermute(tail, axis, [(i, (i + 1) % count) for i in...  21.7 us
    squeeze x128, local copies, waits for them, and re-layouts, on_device(): rows_x[row_index]  9.15 us
  transfers between devices with their start and end apart: 5, of which 2 were waited for; matrix products, arithmetic and copies ran while one was open for 3% of the time, Pallas kernels for 0%

commit v1 on v0

v1 whole, which is shorter than its diff:
```python
import functools

import numpy as np

import jax
import jax.numpy as jnp
from jax import lax
from jax.experimental import pallas as pl
from jax.experimental.pallas import tpu as pltpu
from jax.sharding import PartitionSpec as P

MESH = pl.DeviceIdType.MESH
F32 = jnp.float32
ALPHA = 0.499
COEFS = [
    (193.0 + 126.0 * ALPHA) / 256.0,
    (105.0 + 302.0 * ALPHA) / 256.0,
    15.0 * (2.0 * ALPHA - 1.0) / 64.0,
    45.0 * (1.0 - 2.0 * ALPHA) / 512.0,
    5.0 * (2.0 * ALPHA - 1.0) / 256.0,
    (1.0 - 2.0 * ALPHA) / 512.0,
]
PATCH = 32
SOLVERS = 3


def toeplitz(size, offsets):
    out = np.zeros((size, size))
    for offset, value in offsets.items():
        out += np.diag(np.full(size - abs(offset), value), offset)
    return out


def constants(gx, gy, ny, nx, nz):
    c = {}
    big_y, big_x = gy * ny, gx * nx
    root = (-1.0 + np.sqrt(1.0 - 4.0 * ALPHA**2)) / (2.0 * ALPHA)
    amp = 1.0 / np.sqrt(1.0 - 4.0 * ALPHA**2)
    half = {n: (COEFS[0] if n == 0 else 0.5 * COEFS[n]) for n in range(6)}
    stencil = np.array([half[abs(n)] for n in range(-5, 6)])
    quotient = np.zeros(11)
    rest = stencil.copy()
    for n in range(5, 0, -1):
        q = rest[5 + n] / ALPHA
        for m in {n - 1, 1 - n}:
            quotient[5 + m] += q if m else q
            rest[5 + m - 1 : 5 + m + 2] -= q * np.array([ALPHA, 1.0, ALPHA])
    lam = rest[5]
    cq = {d: quotient[5 + d] for d in range(-4, 5)}
    t_local = np.linalg.inv(toeplitz(ny, {-1: ALPHA, 0: 1.0, 1: ALPHA}))
    inner = toeplitz(ny, cq) + lam * t_local
    c["inner"] = np.kron(np.eye(nz), inner)
    j = np.arange(ny)
    c["pq"] = np.concatenate(
        [np.kron(np.eye(nz), root ** (ny - 1 - j)[None]), np.kron(np.eye(nz), root**j[None])]
    )
    kinds = np.zeros((3, ny, 12))
    for kind in range(3):
        for h in range(4):
            for row in range(ny):
                low, high = h - 4 - row, ny + h - row
                if kind > 0 and abs(low) <= 4:
                    kinds[kind, row, h] = cq[low]
                if kind < 2 and abs(high) <= 4:
                    kinds[kind, row, 4 + h] = cq[high]
        kinds[kind, :, 8] = -lam * ALPHA * t_local[:, 0]
        kinds[kind, :, 9] = -lam * ALPHA * t_local[:, -1]
    edge = np.array([cq[-1 - row] if row < 4 else 0.0 for row in range(ny)])
    kinds[0, :, 8] = ALPHA * edge
    kinds[0, :, 10] = inner[:, 1]
    kinds[2, :, 9] = ALPHA * edge[::-1]
    kinds[2, :, 11] = inner[:, ny - 2]
    c["sides"] = np.stack(
        [np.einsum("ri,zw->zriw", k, np.eye(nz)).reshape(nz * ny, 12 * nz) for k in kinds]
    )
    t_inv = np.linalg.inv(toeplitz(big_y, {-1: ALPHA, 0: 1.0, 1: ALPHA}))
    c["t_inv"], c["root"], c["amp"] = t_inv, root, amp
    third = 1.0 / 3.0
    s = (-1.0 + np.sqrt(1.0 - 4.0 * third**2)) / (2.0 * third)
    amp_x = 1.0 / np.sqrt(1.0 - 4.0 * third**2)
    q_mat = toeplitz(big_x, {1: 7.0 / 9.0, -1: -7.0 / 9.0, 2: 1.0 / 36.0, -2: -1.0 / 36.0})
    p_mat = toeplitz(big_x, {-1: third, 0: 1.0, 1: third})
    d_mat = -np.linalg.solve(p_mat, q_mat.T).T
    c["d_mat"] = d_mat
    c["local"] = np.stack([d_mat[k * nx : (k + 1) * nx, k * nx : (k + 1) * nx].T for k in range(gx)])
    x = np.arange(nx)
    fun = np.zeros((4, nx))
    fun[0], fun[1] = s ** (nx - 1 - x), s**x
    fun[2, 0], fun[3, nx - 1] = 1.0, 1.0
    c["fun"] = np.repeat(fun.T, ny, axis=1)
    c["val"] = np.stack(
        [np.einsum("ri,fx->ixfr", k[:, 8:], fun).reshape(4 * nx, 4 * ny) for k in kinds]
    )
    i = np.arange(-1, nx + 1)
    shape_s, shape_r = amp_x * s ** (i + 1), amp_x * s ** (nx - i)
    shapes = np.zeros((gx, 4, nx))
    for k in range(gx):
        for f, w in ((0, shape_s), (1, shape_r)):
            shapes[k, f] = -25.0 / 36.0 * (w[2:] - w[:-2])
            if k == 0:
                shapes[k, f, 0] += w[1] / 36.0
            if k == gx - 1:
                shapes[k, f, -1] -= w[nx] / 36.0
        shapes[k, 3, 0], shapes[k, 2, -1] = 1.0 / 12.0, -1.0 / 12.0
    c["shapes"] = np.repeat(shapes, ny, axis=1)
    mix = np.zeros((gx, gx, 4, 4))
    norm = 1.0 / (1.0 - s ** (2.0 * (big_x + 1)))
    for k in range(gx):
        for m in range(gx):
            k0, m0 = k * nx, m * nx
            m1 = m0 + nx - 1
            if m < k:
                mix[k, m, 0, 0] = norm * s ** float(k0 - m1 - 1)
                mix[k, m, 0, 1] = norm * s ** float(2 * big_x + 2 - nx - k0 + m0)
            if m > k:
                mix[k, m, 0, 1] = norm * s ** float(m0 - k0 - nx)
                mix[k, m, 0, 0] = norm * s ** float(2 * big_x + 1 + k0 - m1)
            if m != k:
                mix[k, m, 1, 0] = -norm * s ** float(2 * big_x - k0 - nx - m1)
                mix[k, m, 2, 1] = -norm * s ** float(k0 + m0 + 1)
            mix[k, m, 0, 2], mix[k, m, 0, 3] = float(m == k + 1), float(m == k - 1)
    c["mix"] = np.repeat(mix, ny, axis=3)
    b_mat = toeplitz(big_y, {n: half[abs(n)] for n in range(-5, 6)})
    col_sums = (b_mat @ t_inv).reshape(gy, ny, big_y).sum(1)
    groups = gy // 4
    wall = np.zeros((gy, 4, 8, ny))
    for m in range(gy):
        rows = col_sums[:, m * ny : (m + 1) * ny]
        for y in range(gy):
            wall[m, y % 4, y // 4] = rows[y]
        wall[m, 0, 4] = t_inv[0, m * ny : (m + 1) * ny]
        wall[m, 0, 5] = t_inv[-1, m * ny : (m + 1) * ny]
    assert groups <= 4
    c["wall"] = wall.reshape(gy, 32, ny)
    ends = np.zeros((2, 4, 8))
    for y in range(gy):
        ends[0, y % 4, y // 4], ends[1, y % 4, y // 4] = col_sums[y, 1], col_sums[y, -2]
    c["ends"] = np.repeat(ends.reshape(2, 32, 1), 128, axis=2)
    patch = np.zeros((gx, nx, 4, 32))
    sums = d_mat.reshape(big_x // PATCH, PATCH, big_x).sum(1)
    for k in range(gx):
        patch[k, :, :, : sums.shape[0]] = sums[:, k * nx : (k + 1) * nx].T[:, None, :]
    c["patch"] = patch.reshape(gx, nx, 128)
    return c


def dot(a, b):
    return jnp.dot(a, b, preferred_element_type=F32, precision=lax.Precision.HIGHEST)


def kernel(
    sizes, cst,
    cot_h, closure_h, owner_h, blow_h,
    inner_h, pq_h, sides_h, fun_h, val_h, local_h, shapes_h, mix_h, wall_h, ends_h, patch_h,
    grad_o, act_o,
    cot, closure, owner, blow, inner, pq, sides, fun, val, local, shapes, mix, wall, ends, patch,
    pq_out, pq_in, halo_out, halo_in, v_out, v_in, w_out, w_in, tot_out, tot_in, x_out, x_in,
    load_sem, send_sem, recv_sem, v_sem,
):
    gx_n, gy_n, gz_n, ny, nx, nz = sizes
    gx, gy, gz = (lax.axis_index(a) for a in ("gx", "gy", "gz"))
    big_y = gy_n * ny
    planes = 3 * nz

    barrier = pltpu.get_barrier_semaphore()

    def greet(**where):
        pl.semaphore_signal(barrier, inc=1, device_id=where, device_id_type=MESH)

    def load(k, src, dst):
        copy = pltpu.make_async_copy(src, dst, load_sem.at[k])
        copy.start()
        return copy

    first = [load(0, cot_h, cot), load(1, pq_h, pq)]
    for d in range(1, gx_n):
        greet(gx=lax.rem(gx + d, gx_n))
    for d in (1, gy_n - 1):
        greet(gy=lax.rem(gy + d, gy_n))

    @pl.when(gy < SOLVERS)
    def _():
        for d in range(1, gy_n):
            greet(gy=lax.rem(gy + d, gy_n))

    @pl.when(gy == 0)
    def _():
        for d in range(1, gy_n):
            greet(gy=lax.rem(gy + d, gy_n), gz=0)

        @pl.when(gz != 0)
        def _():
            greet(gz=0)

    kind = jnp.where(gy == 0, 0, jnp.where(gy == gy_n - 1, 2, 1))
    rest = [
        load(2, closure_h, closure), load(3, owner_h, owner), load(4, wall_h.at[gy], wall),
        load(5, ends_h, ends), load(6, patch_h.at[gx], patch), load(7, inner_h, inner),
        load(8, sides_h.at[kind], sides), load(9, fun_h, fun), load(10, val_h.at[kind], val),
        load(11, local_h.at[gx], local), load(12, shapes_h.at[gx], shapes), load(13, mix_h.at[gx], mix),
        load(14, blow_h, blow),
    ]

    for copy in first:
        copy.wait()
    for c in range(3):
        pair = dot(pq[...], cot[c * nz * ny : (c + 1) * nz * ny, :])
        pq_out[c, 0] = pair[:nz]
        pq_out[c, 1] = pair[nz:]

    n_wait = (gx_n - 1) + 2 + SOLVERS - (gy < SOLVERS).astype(jnp.int32)
    n_wait += jnp.where(gz == 0, gz_n - (gy == 0).astype(jnp.int32), 0)
    pl.semaphore_wait(barrier, n_wait)

    def pq_copy(c):
        return pltpu.make_async_remote_copy(
            src_ref=pq_out.at[c], dst_ref=pq_in.at[gy], send_sem=send_sem.at[c], recv_sem=recv_sem.at[0],
            device_id={"gy": c}, device_id_type=MESH)

    for c in range(SOLVERS):
        @pl.when(gy != c)
        def _():
            pq_copy(c).start()

        @pl.when(gy == c)
        def _():
            pq_in[gy] = pq_out[c]

    for r in range(4):
        for c in range(3):
            base = c * nz * ny
            halo_out[0, r, c * nz : (c + 1) * nz] = cot[pl.ds(base + ny - 4 + r, nz, stride=ny), :]
            halo_out[1, r, c * nz : (c + 1) * nz] = cot[pl.ds(base + r, nz, stride=ny), :]

    def halo_copy(side):
        return pltpu.make_async_remote_copy(
            src_ref=halo_out.at[side], dst_ref=halo_in.at[side], send_sem=send_sem.at[3 + side],
            recv_sem=recv_sem.at[1 + side],
            device_id={"gy": lax.rem(gy + (1 if side == 0 else gy_n - 1), gy_n)}, device_id_type=MESH)

    for side in (0, 1):
        halo_copy(side).start()

    for copy in rest:
        copy.wait()
    deltas = []
    for side in (0, 1):
        deltas.append(ALPHA - (0.5 * ALPHA) * closure[side].astype(F32))
    delta0, delta1 = deltas
    tau, eps = float(cst["t_inv"][0, 1]), float(cst["t_inv"][0, big_y - 2])

    def ends_of(y0, y1, d0, d1):
        p0, p1 = 1.0 - tau * d0, 1.0 - tau * d1
        scale = 1.0 / (p0 * p1 - (eps * eps) * (d0 * d1))
        return (p1 * y0 + eps * (d1 * y1)) * scale, (p0 * y1 + eps * (d0 * y0)) * scale

    lane = lax.broadcasted_iota(jnp.int32, (8, 128), 1)
    row = lax.broadcasted_iota(jnp.int32, (8, 128), 0)

    def wall_copy(z):
        return pltpu.make_async_remote_copy(
            src_ref=w_out, dst_ref=w_in.at[gy], send_sem=send_sem.at[5 + z], recv_sem=recv_sem.at[3],
            device_id={"gy": 0, "gz": z}, device_id_type=MESH)

    @pl.when(gz == 0)
    def _():
        blend = sum(blow[c] * cot[c * nz * ny : c * nz * ny + ny, :] for c in range(3))
        parts = dot(wall[...], blend)
        x0, x1 = ends_of(parts[4:5], parts[5:6], delta0[0:1], delta1[0:1])
        parts = parts + ends[0] * (delta0[0:1] * x0) + ends[1] * (delta1[0:1] * x1)
        spread = dot(parts, patch[...])
        total = jnp.zeros((8, 128), F32)
        for q in range(4):
            total += jnp.where((lane // 32 == q) & (row < 4), spread[8 * q : 8 * q + 8], 0.0)
        at = (row == 4 + gy // 4) & (lane // 32 == lax.rem(gy, 4))
        for q in range(nx // PATCH):
            owned = owner[0:1, q * PATCH : q * PATCH + 1].astype(F32)
            total += jnp.where(at & (lane % 32 == gx * (nx // PATCH) + q), owned, 0.0)
        w_out[...] = total
        for z in range(gz_n):
            if z == 0:
                @pl.when(gy != 0)
                def _():
                    wall_copy(0).start()

                @pl.when(gy == 0)
                def _():
                    w_in[0] = w_out[...]
            else:
                wall_copy(z).start()

    u = [dot(inner[...], cot[c * nz * ny : (c + 1) * nz * ny, :]) for c in range(3)]
    for c in range(3):
        grad_o[c * nz * ny : (c + 1) * nz * ny, :] = u[c]

    def v_copy(c, k):
        return pltpu.make_async_remote_copy(
            src_ref=v_out.at[k], dst_ref=v_in.at[c], send_sem=send_sem.at[9], recv_sem=v_sem.at[c],
            device_id={"gy": k}, device_id_type=MESH)

    root, amp, t_inv = cst["root"], cst["amp"], cst["t_inv"]

    @pl.when(gy < SOLVERS)
    def _():
        pltpu.make_async_remote_copy(
            src_ref=pq_in.at[0 : gy_n - 1], dst_ref=pq_in.at[0 : gy_n - 1], send_sem=send_sem.at[0],
            recv_sem=recv_sem.at[0], device_id={"gy": 0}, device_id_type=MESH).wait_recv()
        hop = float(root**ny)
        before, after = [None] * gy_n, [None] * gy_n
        run = jnp.zeros((nz, nx), F32)
        for m in range(gy_n):
            before[m] = run
            run = hop * run + pq_in[m, 0]
        p_all = run
        run = jnp.zeros((nz, nx), F32)
        for m in reversed(range(gy_n)):
            after[m] = run
            run = hop * run + pq_in[m, 1]
        q_all = run
        far = float(root ** (big_y + 1))
        norm = -amp / (1.0 - far * far)
        a = float(norm * root) * (q_all - far * p_all)
        b = float(norm * root) * (p_all - far * q_all)
        y0 = float(amp) * q_all + float(root) * a + float(root**big_y) * b
        y1 = float(amp) * p_all + float(root**big_y) * a + float(root) * b
        x0, x1 = ends_of(y0, y1, delta0, delta1)
        w0, w1 = delta0 * x0, delta1 * x1

        def at(i, value):
            value = float(amp) * value + float(root ** (i + 1)) * a + float(root ** (big_y - i)) * b
            return value + float(t_inv[i, 1]) * w0 + float(t_inv[i, big_y - 2]) * w1

        for k in range(gy_n):
            if k == 0:
                v_out[k, 0] = x0
            else:
                v_out[k, 0] = at(k * ny - 1, before[k] + float(root) * (hop * after[k] + pq_in[k, 1]))
            if k == gy_n - 1:
                v_out[k, 1] = x1
            else:
                v_out[k, 1] = at((k + 1) * ny, float(root) * (hop * before[k] + pq_in[k, 0]) + after[k])
            for c in range(SOLVERS):
                if c == k:
                    @pl.when(gy == c)
                    def _():
                        v_in[c] = v_out[k]
                else:
                    @pl.when(gy == c)
                    def _():
                        v_copy(c, k).start()

    def tot_copy(k):
        return pltpu.make_async_remote_copy(
            src_ref=tot_out, dst_ref=tot_in, send_sem=send_sem.at[10], recv_sem=recv_sem.at[4],
            device_id={"gy": k}, device_id_type=MESH)

    @pl.when(gy == 0)
    def _():
        @pl.when(gz == 0)
        def _():
            pltpu.make_async_remote_copy(
                src_ref=w_in.at[1:gy_n], dst_ref=w_in.at[1:gy_n], send_sem=send_sem.at[5],
                recv_sem=recv_sem.at[3], device_id={"gy": 0}, device_id_type=MESH).wait_recv()

        @pl.when(gz != 0)
        def _():
            pltpu.make_async_remote_copy(
                src_ref=w_in, dst_ref=w_in, send_sem=send_sem.at[5],
                recv_sem=recv_sem.at[3], device_id={"gy": 0}, device_id_type=MESH).wait_recv()
        total = w_in[0]
        for m in range(1, gy_n):
            total = total + w_in[m]
        tot_out[...] = total
        tot_in[...] = total
        for k in range(1, gy_n):
            tot_copy(k).start()

    for side in (0, 1):
        halo_copy(side).wait_recv()
    same_row = (
        lax.broadcasted_iota(jnp.int32, (nz * ny, 128), 0) % ny
        == lax.broadcasted_iota(jnp.int32, (nz * ny, 128), 1) % ny
    )
    plane_of = (
        lax.broadcasted_iota(jnp.int32, (nz, nz * ny), 1) // ny
        == lax.broadcasted_iota(jnp.int32, (nz, nz * ny), 0)
    ).astype(F32)
    x0_parts = []
    for c in range(3):
        rows = halo_in[:, :, c * nz : (c + 1) * nz, :].reshape(8 * nz, nx)
        u_c = grad_o[c * nz * ny : (c + 1) * nz * ny, :] + dot(sides[:, : 8 * nz], rows)
        grad_o[c * nz * ny : (c + 1) * nz * ny, :] = u_c
        x0_parts.append(dot(plane_of, jnp.where(same_row, dot(u_c, fun[...]), 0.0)))

    for c in range(SOLVERS):
        @pl.when(gy != c)
        def _():
            v_copy(c, 0).wait_recv()

    v_rows = []
    for c in range(3):
        low, high = v_in[c, 0], v_in[c, 1]
        v_rows.append([low, high, delta0 * low, delta1 * high])
        x_out[c * nz : (c + 1) * nz] = x0_parts[c] + dot(jnp.concatenate(v_rows[c], axis=1), val[...])

    @pl.when(gy != 0)
    def _():
        tot_copy(0).wait_recv()

    x_out[planes : planes + 8] = tot_in[...]

    def x_copy(d):
        return pltpu.make_async_remote_copy(
            src_ref=x_out, dst_ref=x_in.at[gx], send_sem=send_sem.at[11], recv_sem=recv_sem.at[5],
            device_id={"gx": lax.rem(gx + d, gx_n)}, device_id_type=MESH)

    for d in range(1, gx_n):
        x_copy(d).start()
    x_in[gx] = x_out[...]

    for c in range(3):
        u_c = grad_o[c * nz * ny : (c + 1) * nz * ny, :] + dot(
            sides[:, 8 * nz :], jnp.concatenate(v_rows[c], axis=0))
        grad_o[c * nz * ny : (c + 1) * nz * ny, :] = dot(u_c, local[...])

    pltpu.make_async_remote_copy(
        src_ref=x_in.at[0 : gx_n - 1], dst_ref=x_in.at[0 : gx_n - 1], send_sem=send_sem.at[11],
        recv_sem=recv_sem.at[5], device_id={"gx": 0}, device_id_type=MESH).wait_recv()
    for c in range(3):
        value, to_r, to_p = (jnp.zeros((nz, 128), F32) for _ in range(3))
        for m in range(gx_n):
            part = x_in[m, c * nz : (c + 1) * nz]
            value += mix[m, 0:1] * part
            to_r += mix[m, 1:2] * part
            to_p += mix[m, 2:3] * part
        value += pltpu.roll(to_r, ny, 1) + pltpu.roll(to_p, 128 - ny, 1)
        spread = jnp.broadcast_to(value[:, None, :], (nz, ny, 128)).reshape(nz * ny, 128)
        spread = jnp.where(same_row, spread, 0.0)
        grad_o[c * nz * ny : (c + 1) * nz * ny, :] += dot(spread, shapes[...])
    total = x_in[0, planes : planes + 8]
    for m in range(1, gx_n):
        total = total + x_in[m, planes : planes + 8]
    mine = ((gx * gy_n + gy) * gz_n + gz).astype(F32)
    hit = (pltpu.roll(total, 4, 0) == mine) & (row < gy_n // 4) & (lane % 32 < gx_n * nx // PATCH)
    act_o[...] = jnp.sum(jnp.where(hit, total, 0.0), keepdims=True)

    for c in range(SOLVERS):
        @pl.when(gy != c)
        def _():
            pq_copy(c).wait_send()
    for side in (0, 1):
        halo_copy(side).wait_send()

    @pl.when(gz == 0)
    def _():
        for z in range(1, gz_n):
            wall_copy(z).wait_send()

        @pl.when(gy != 0)
        def _():
            wall_copy(0).wait_send()

    @pl.when(gy < SOLVERS)
    def _():
        pltpu.make_async_remote_copy(
            src_ref=v_out.at[0 : gy_n - 1], dst_ref=v_out.at[0 : gy_n - 1], send_sem=send_sem.at[9],
            recv_sem=v_sem.at[0], device_id={"gy": 0}, device_id_type=MESH).wait_send()

    @pl.when(gy == 0)
    def _():
        for k in range(1, gy_n):
            tot_copy(k).wait_send()

    for d in range(1, gx_n):
        x_copy(d).wait_send()


def on_device(sizes, cst, cotangent, closure, owner, blowing):
    gx_n, gy_n, gz_n, ny, nx, nz = sizes
    f32 = lambda name: jnp.asarray(np.asarray(cst[name], np.float32))
    tables = [f32(n) for n in ("inner", "pq", "sides", "fun", "val", "local", "shapes", "mix", "wall", "ends", "patch")]
    anyspec = pl.BlockSpec(memory_space=pltpu.HBM)
    vmem = pl.BlockSpec(memory_space=pltpu.VMEM)
    v = lambda *shape: pltpu.VMEM(shape, F32)
    rows = 3 * nz * ny
    scratch = [
        v(rows, nx), pltpu.VMEM((2, nz, nx), jnp.int32), pltpu.VMEM((ny, nx), jnp.int32), pltpu.SMEM((3,), F32),
        v(nz * ny, nz * ny), v(2 * nz, nz * ny), v(nz * ny, 12 * nz), v(nx, 128), v(4 * nx, 128),
        v(nx, nx), v(128, nx), v(gx_n, 4, 128), v(32, ny), v(2, 32, 128), v(nx, 128),
        v(3, 2, nz, nx), v(gy_n, 2, nz, nx), v(2, 4, 3 * nz, nx), v(2, 4, 3 * nz, nx),
        v(gy_n, 2, nz, nx), v(3, 2, nz, nx), v(8, 128), v(gy_n, 8, 128), v(8, 128), v(8, 128),
        v(3 * nz + 8, 128), v(gx_n, 3 * nz + 8, 128),
        pltpu.SemaphoreType.DMA((15,)), pltpu.SemaphoreType.DMA((12,)), pltpu.SemaphoreType.DMA((6,)),
        pltpu.SemaphoreType.DMA((3,)),
    ]
    gradient, share = pl.pallas_call(
        functools.partial(kernel, sizes, cst),
        out_shape=(jax.ShapeDtypeStruct((rows, nx), F32), jax.ShapeDtypeStruct((1, 1), F32)),
        in_specs=[anyspec] * (4 + len(tables)),
        out_specs=(vmem, vmem),
        scratch_shapes=scratch,
        compiler_params=pltpu.CompilerParams(
            collective_id=0, has_side_effects=True, vmem_limit_bytes=64 * 1024 * 1024
        ),
    )(cotangent.reshape(rows, nx), jnp.transpose(closure, (0, 2, 1)), owner.T, blowing, *tables)
    return gradient.reshape(cotangent.shape), share.reshape(1)


def solution(mesh):
    gx_n, gy_n, gz_n = (mesh.shape[a] for a in ("gx", "gy", "gz"))
    sizes = (gx_n, gy_n, gz_n, 512 // 16, 1024 // 8, 32 // 4)
    cst = constants(gx_n, gy_n, sizes[3], sizes[4], sizes[5])
    in_specs = (P(None, "gz", "gy", "gx"), P(None, "gx", "gz"), P("gx", "gy"), P())
    out_specs = (P(None, "gz", "gy", "gx"), P(("gx", "gy", "gz")))
    return jax.shard_map(
        functools.partial(on_device, sizes, cst),
        mesh=mesh, in_specs=in_specs, out_specs=out_specs, check_vma=False,
    )
```

time: 365 us -> 34.6 us (0.09)
  blocking collectives: 167 us -> 0 us
  waiting for transfers between devices: 75.3 us -> 0 us
  other arithmetic: 46.7 us -> 0 us
  local copies, waits for them, and re-layouts: 46.8 us -> 1.77 us
  Pallas kernels: 0 us -> 30.3 us
  between operations: 16.4 us -> 2.39 us
  starting transfers between devices: 10.3 us -> 0 us
    unnamed x1 -> x0, blocking collectives: 99.7 us -> none
    all_gather x1 -> x0, waiting for transfers between devices: 73.1 us -> none  [prefix_2(): everything = lax.all_gather(value, axis)]
    all_gather x3 -> x0, blocking collectives: 67 us -> none  [prefix_2(): everything = lax.all_gather(value, axis)]
    div x52 -> x0, other arithmetic: 32 us -> none  [rescaled(): return [entry / largest for entry in entries]]
    pallas_call x0 -> x1, Pallas kernels: none -> 30.3 us  [on_device(): pl.pallas_call(functools.partial(kernel, sizes, cst), out_shape=(jax.Shap...]
    concatenate x14 -> x0, local copies, waits for them, and re-layouts: 21.7 us -> none  [padded_2(): jnp.concatenate([lax.ppermute(tail, axis, [(i, (i + 1) % count) for i in...]
    ppermute x4 -> x0, starting transfers between devices: 10.2 us -> none  [the longest x2 7.03 us: padded_2(): lax.ppermute(tail, axis, [(i, (i + 1) % count) for i in range(ends)])]
    squeeze x128 -> x0, local copies, waits for them, and re-layouts: 9.15 us -> none  [on_device(): rows_x[row_index]]
  transfers between devices with their start and end apart: 5 -> 0, of which waited for: 2 -> 0; matrix products, arithmetic and copies ran while one was open for 3% -> 0% of each run, Pallas kernels for 0% -> 0%
where the time goes in v1:
time: 34.6 us; the launch traced here: 34.4 us
  Pallas kernels  30.3 us (88%)
  between operations  2.39 us (7%)
  local copies, waits for them, and re-layouts  1.77 us (5%)
    pallas_call x1, Pallas kernels, on_device(): pl.pallas_call(functools.partial(kernel, sizes, cst), out_shape=(jax.Shap...  30.3 us
    unnamed x1, local copies, waits for them, and re-layouts  1.77 us

profile of v1, /device:TPU:1, one launch (start us, length us, event | category | flops | bytes accessed | tf_op | source)
XLA Modules:
  0.0 34.4 jit_solution(12692690942758531042)
XLA Ops:
  0.6 30.3 %shard_map.158 = (f32[768,128]{1,0:T(8,128)}, f32[1,1]{1,0:T(1,128)}) custom-call(f32[768,128]{1,0:T(8,128)} %bitcast.5, s32[2,8,128]{2,1,0:T(8,128)} %bitcast.8, s32[32,128]{1,0:T(8,128)} %bitcast.7, f32[3]{0:T(128)} %blow_h.1, f32[256,256]{1,0:T(8,128)} %constant.22.clone.inner_h, f32[16,256]{1,0:T(8,128)} %constant.23.clone.pq_h, ...), custom_call_target="tpu_custom_call" | custom-call | tf_op jit(solution)/shard_map/pallas_call | solution.py:496
  30.9 1.8 %copy.19 = f32[3,8,32,128]{3,2,1,0:T(8,128)} copy(f32[3,8,32,128]{3,2,1,0:T(8,128)} %bitcast.6) | data formatting | bytes 786432

commit v2 on v1

--- a/solution.py
+++ b/solution.py
@@ -21,7 +21,6 @@
     (1.0 - 2.0 * ALPHA) / 512.0,
 ]
 PATCH = 32
-SOLVERS = 3
 
 
 def toeplitz(size, offsets):
@@ -151,11 +150,11 @@
 def kernel(
     sizes, cst,
     cot_h, closure_h, owner_h, blow_h,
-    inner_h, pq_h, sides_h, fun_h, val_h, local_h, shapes_h, mix_h, wall_h, ends_h, patch_h,
-    grad_o, act_o,
-    cot, closure, owner, blow, inner, pq, sides, fun, val, local, shapes, mix, wall, ends, patch,
-    pq_out, pq_in, halo_out, halo_in, v_out, v_in, w_out, w_in, tot_out, tot_in, x_out, x_in,
-    load_sem, send_sem, recv_sem, v_sem,
+    inner_h, pq_h, sides_h, fun_h, val_h, local_h, mix_h, wall_h, ends_h, patch_h,
+    grad_o, small_o,
+    cot, closure, owner, blow, inner, pq, sides, fun, val, local, mix, wall, ends, patch,
+    pq_out, pq_in, halo_out, halo_in, v_out, v_in, w_out, w_in, tot_out, tot_in, x_out, x_in, sum_in, own,
+    load_sem, send_sem, recv_sem,
 ):
     gx_n, gy_n, gz_n, ny, nx, nz = sizes
     gx, gy, gz = (lax.axis_index(a) for a in ("gx", "gy", "gz"))
@@ -178,15 +177,11 @@
     for d in (1, gy_n - 1):
         greet(gy=lax.rem(gy + d, gy_n))
 
-    @pl.when(gy < SOLVERS)
-    def _():
-        for d in range(1, gy_n):
-            greet(gy=lax.rem(gy + d, gy_n))
-
     @pl.when(gy == 0)
     def _():
-        for d in range(1, gy_n):
-            greet(gy=lax.rem(gy + d, gy_n), gz=0)
+        for k in range(1, gy_n):
+            greet(gy=k)
+            greet(gy=k, gz=0)
 
         @pl.when(gz != 0)
         def _():
@@ -197,7 +192,7 @@
         load(2, closure_h, closure), load(3, owner_h, owner), load(4, wall_h.at[gy], wall),
         load(5, ends_h, ends), load(6, patch_h.at[gx], patch), load(7, inner_h, inner),
         load(8, sides_h.at[kind], sides), load(9, fun_h, fun), load(10, val_h.at[kind], val),
-        load(11, local_h.at[gx], local), load(12, shapes_h.at[gx], shapes), load(13, mix_h.at[gx], mix),
+        load(11, local_h.at[gx], local), load(13, mix_h.at[gx], mix),
         load(14, blow_h, blow),
     ]
 
@@ -207,39 +202,6 @@
         pair = dot(pq[...], cot[c * nz * ny : (c + 1) * nz * ny, :])
         pq_out[c, 0] = pair[:nz]
         pq_out[c, 1] = pair[nz:]
-
-    n_wait = (gx_n - 1) + 2 + SOLVERS - (gy < SOLVERS).astype(jnp.int32)
-    n_wait += jnp.where(gz == 0, gz_n - (gy == 0).astype(jnp.int32), 0)
-    pl.semaphore_wait(barrier, n_wait)
-
-    def pq_copy(c):
-        return pltpu.make_async_remote_copy(
-            src_ref=pq_out.at[c], dst_ref=pq_in.at[gy], send_sem=send_sem.at[c], recv_sem=recv_sem.at[0],
-            device_id={"gy": c}, device_id_type=MESH)
-
-    for c in range(SOLVERS):
-        @pl.when(gy != c)
-        def _():
-            pq_copy(c).start()
-
-        @pl.when(gy == c)
-        def _():
-            pq_in[gy] = pq_out[c]
-
-    for r in range(4):
-        for c in range(3):
-            base = c * nz * ny
-            halo_out[0, r, c * nz : (c + 1) * nz] = cot[pl.ds(base + ny - 4 + r, nz, stride=ny), :]
-            halo_out[1, r, c * nz : (c + 1) * nz] = cot[pl.ds(base + r, nz, stride=ny), :]
-
-    def halo_copy(side):
-        return pltpu.make_async_remote_copy(
-            src_ref=halo_out.at[side], dst_ref=halo_in.at[side], send_sem=send_sem.at[3 + side],
-            recv_sem=recv_sem.at[1 + side],
-            device_id={"gy": lax.rem(gy + (1 if side == 0 else gy_n - 1), gy_n)}, device_id_type=MESH)
-
-    for side in (0, 1):
-        halo_copy(side).start()
 
     for copy in rest:
         copy.wait()
@@ -259,7 +221,7 @@
 
     def wall_copy(z):
         return pltpu.make_async_remote_copy(
-            src_ref=w_out, dst_ref=w_in.at[gy], send_sem=send_sem.at[5 + z], recv_sem=recv_sem.at[3],
+            src_ref=w_out.at[0:5], dst_ref=w_in.at[gy, 0:5], send_sem=send_sem.at[5 + z], recv_sem=recv_sem.at[3],
             device_id={"gy": 0, "gz": z}, device_id_type=MESH)
 
     @pl.when(gz == 0)
@@ -272,11 +234,18 @@
         total = jnp.zeros((8, 128), F32)
         for q in range(4):
             total += jnp.where((lane // 32 == q) & (row < 4), spread[8 * q : 8 * q + 8], 0.0)
-        at = (row == 4 + gy // 4) & (lane // 32 == lax.rem(gy, 4))
+        at = (row == 4) & (lane // 32 == lax.rem(gy, 4))
         for q in range(nx // PATCH):
             owned = owner[0:1, q * PATCH : q * PATCH + 1].astype(F32)
             total += jnp.where(at & (lane % 32 == gx * (nx // PATCH) + q), owned, 0.0)
         w_out[...] = total
+
+    n_wait = (gx_n - 1) + 2 + (gy != 0).astype(jnp.int32)
+    n_wait += jnp.where(gz == 0, gz_n - (gy == 0).astype(jnp.int32), 0)
+    pl.semaphore_wait(barrier, n_wait)
+
+    @pl.when(gz == 0)
+    def _():
         for z in range(gz_n):
             if z == 0:
                 @pl.when(gy != 0)
@@ -289,65 +258,92 @@
             else:
                 wall_copy(z).start()
 
-    u = [dot(inner[...], cot[c * nz * ny : (c + 1) * nz * ny, :]) for c in range(3)]
-    for c in range(3):
-        grad_o[c * nz * ny : (c + 1) * nz * ny, :] = u[c]
-
-    def v_copy(c, k):
-        return pltpu.make_async_remote_copy(
-            src_ref=v_out.at[k], dst_ref=v_in.at[c], send_sem=send_sem.at[9], recv_sem=v_sem.at[c],
+    def pq_copy():
+        return pltpu.make_async_remote_copy(
+            src_ref=pq_out, dst_ref=pq_in.at[gy], send_sem=send_sem.at[0], recv_sem=recv_sem.at[0],
+            device_id={"gy": 0}, device_id_type=MESH)
+
+    @pl.when(gy != 0)
+    def _():
+        pq_copy().start()
+
+    @pl.when(gy == 0)
+    def _():
+        pq_in[0] = pq_out[...]
+
+    for c in range(3):
+        own[c * nz * ny : (c + 1) * nz * ny, :] = dot(inner[...], cot[c * nz * ny : (c + 1) * nz * ny, :])
+
+    for r in range(4):
+        for c in range(3):
+            base = c * nz * ny
+            halo_out[0, r, c * nz : (c + 1) * nz] = cot[pl.ds(base + ny - 4 + r, nz, stride=ny), :]
+            halo_out[1, r, c * nz : (c + 1) * nz] = cot[pl.ds(base + r, nz, stride=ny), :]
+
+    def halo_copy(side):
+        return pltpu.make_async_remote_copy(
+            src_ref=halo_out.at[side], dst_ref=halo_in.at[side], send_sem=send_sem.at[3 + side],
+            recv_sem=recv_sem.at[1 + side],
+            device_id={"gy": lax.rem(gy + (1 if side == 0 else gy_n - 1), gy_n)}, device_id_type=MESH)
+
+    for side in (0, 1):
+        halo_copy(side).start()
+
+    def v_copy(k):
+        return pltpu.make_async_remote_copy(
+            src_ref=v_out.at[k], dst_ref=v_in, send_sem=send_sem.at[9], recv_sem=recv_sem.at[6],
             device_id={"gy": k}, device_id_type=MESH)
 
     root, amp, t_inv = cst["root"], cst["amp"], cst["t_inv"]
 
-    @pl.when(gy < SOLVERS)
+    @pl.when(gy == 0)
     def _():
         pltpu.make_async_remote_copy(
-            src_ref=pq_in.at[0 : gy_n - 1], dst_ref=pq_in.at[0 : gy_n - 1], send_sem=send_sem.at[0],
+            src_ref=pq_in.at[1:gy_n], dst_ref=pq_in.at[1:gy_n], send_sem=send_sem.at[0],
             recv_sem=recv_sem.at[0], device_id={"gy": 0}, device_id_type=MESH).wait_recv()
         hop = float(root**ny)
-        before, after = [None] * gy_n, [None] * gy_n
-        run = jnp.zeros((nz, nx), F32)
-        for m in range(gy_n):
-            before[m] = run
-            run = hop * run + pq_in[m, 0]
-        p_all = run
-        run = jnp.zeros((nz, nx), F32)
-        for m in reversed(range(gy_n)):
-            after[m] = run
-            run = hop * run + pq_in[m, 1]
-        q_all = run
         far = float(root ** (big_y + 1))
         norm = -amp / (1.0 - far * far)
-        a = float(norm * root) * (q_all - far * p_all)
-        b = float(norm * root) * (p_all - far * q_all)
-        y0 = float(amp) * q_all + float(root) * a + float(root**big_y) * b
-        y1 = float(amp) * p_all + float(root**big_y) * a + float(root) * b
-        x0, x1 = ends_of(y0, y1, delta0, delta1)
-        w0, w1 = delta0 * x0, delta1 * x1
-
-        def at(i, value):
-            value = float(amp) * value + float(root ** (i + 1)) * a + float(root ** (big_y - i)) * b
-            return value + float(t_inv[i, 1]) * w0 + float(t_inv[i, big_y - 2]) * w1
-
+        sums = []
+        for c in range(3):
+            before, after = [None] * gy_n, [None] * gy_n
+            run = jnp.zeros((nz, nx), F32)
+            for m in range(gy_n):
+                before[m] = run
+                run = hop * run + pq_in[m, c, 0]
+            p_all = run
+            run = jnp.zeros((nz, nx), F32)
+            for m in reversed(range(gy_n)):
+                after[m] = run
+                run = hop * run + pq_in[m, c, 1]
+            q_all = run
+            a = float(norm * root) * (q_all - far * p_all)
+            b = float(norm * root) * (p_all - far * q_all)
+            y0 = float(amp) * q_all + float(root) * a + float(root**big_y) * b
+            y1 = float(amp) * p_all + float(root**big_y) * a + float(root) * b
+            sums.append((before, after, a, b) + ends_of(y0, y1, delta0, delta1))
         for k in range(gy_n):
-            if k == 0:
-                v_out[k, 0] = x0
-            else:
-                v_out[k, 0] = at(k * ny - 1, before[k] + float(root) * (hop * after[k] + pq_in[k, 1]))
-            if k == gy_n - 1:
-                v_out[k, 1] = x1
-            else:
-                v_out[k, 1] = at((k + 1) * ny, float(root) * (hop * before[k] + pq_in[k, 0]) + after[k])
-            for c in range(SOLVERS):
-                if c == k:
-                    @pl.when(gy == c)
-                    def _():
-                        v_in[c] = v_out[k]
+            for c in range(3):
+                before, after, a, b, x0, x1 = sums[c]
+
+                def at(i, value):
+                    value = float(amp) * value + float(root ** (i + 1)) * a + float(root ** (big_y - i)) * b
+                    return value + float(t_inv[i, 1]) * (delta0 * x0) + float(t_inv[i, big_y - 2]) * (delta1 * x1)
+
+                low = x0 if k == 0 else at(k * ny - 1, before[k] + float(root) * (hop * after[k] + pq_in[k, c, 1]))
+                high = x1 if k == gy_n - 1 else at(
+                    (k + 1) * ny, float(root) * (hop * before[k] + pq_in[k, c, 0]) + after[k])
+                if k == 0:
+                    v_in[c, 0], v_in[c, 1] = low, high
                 else:
-                    @pl.when(gy == c)
-                    def _():
-                        v_copy(c, k).start()
+                    v_out[k, c, 0], v_out[k, c, 1] = low, high
+            if k:
+                v_copy(k).start()
+
+    def sum_copy(d):
+        return pltpu.make_async_remote_copy(
+            src_ref=tot_in, dst_ref=sum_in.at[gx], send_sem=send_sem.at[12], recv_sem=recv_sem.at[7],
+            device_id={"gx": lax.rem(gx + d, gx_n)}, device_id_type=MESH)
 
     def tot_copy(k):
         return pltpu.make_async_remote_copy(
@@ -359,21 +355,28 @@
         @pl.when(gz == 0)
         def _():
             pltpu.make_async_remote_copy(
-                src_ref=w_in.at[1:gy_n], dst_ref=w_in.at[1:gy_n], send_sem=send_sem.at[5],
+                src_ref=w_in.at[1:gy_n, 0:5], dst_ref=w_in.at[1:gy_n, 0:5], send_sem=send_sem.at[5],
                 recv_sem=recv_sem.at[3], device_id={"gy": 0}, device_id_type=MESH).wait_recv()
 
         @pl.when(gz != 0)
         def _():
             pltpu.make_async_remote_copy(
-                src_ref=w_in, dst_ref=w_in, send_sem=send_sem.at[5],
+                src_ref=w_in.at[:, 0:5], dst_ref=w_in.at[:, 0:5], send_sem=send_sem.at[5],
                 recv_sem=recv_sem.at[3], device_id={"gy": 0}, device_id_type=MESH).wait_recv()
-        total = w_in[0]
-        for m in range(1, gy_n):
-            total = total + w_in[m]
+        total = jnp.zeros((8, 128), F32)
+        for q in range(gy_n // 4):
+            group = w_in[4 * q]
+            for m in range(4 * q + 1, 4 * q + 4):
+                group = group + w_in[m]
+            total = total + jnp.where(row < 4, group, 0.0)
+            total = total + pltpu.roll(jnp.where(row == 4, group, 0.0), q, 0)
         tot_out[...] = total
         tot_in[...] = total
         for k in range(1, gy_n):
             tot_copy(k).start()
+        for d in range(1, gx_n):
+            sum_copy(d).start()
+        sum_in[gx] = tot_in[...]
 
     for side in (0, 1):
         halo_copy(side).wait_recv()
@@ -385,29 +388,27 @@
         lax.broadcasted_iota(jnp.int32, (nz, nz * ny), 1) // ny
         == lax.broadcasted_iota(jnp.int32, (nz, nz * ny), 0)
     ).astype(F32)
-    x0_parts = []
     for c in range(3):
         rows = halo_in[:, :, c * nz : (c + 1) * nz, :].reshape(8 * nz, nx)
-        u_c = grad_o[c * nz * ny : (c + 1) * nz * ny, :] + dot(sides[:, : 8 * nz], rows)
-        grad_o[c * nz * ny : (c + 1) * nz * ny, :] = u_c
-        x0_parts.append(dot(plane_of, jnp.where(same_row, dot(u_c, fun[...]), 0.0)))
-
-    for c in range(SOLVERS):
-        @pl.when(gy != c)
-        def _():
-            v_copy(c, 0).wait_recv()
+        u_c = own[c * nz * ny : (c + 1) * nz * ny, :] + dot(sides[:, : 8 * nz], rows)
+        own[c * nz * ny : (c + 1) * nz * ny, :] = u_c
+        x_out[c * nz : (c + 1) * nz] = dot(plane_of, jnp.where(same_row, dot(u_c, fun[...]), 0.0))
+
+    @pl.when(gy != 0)
+    def _():
+        v_copy(0).wait_recv()
 
     v_rows = []
     for c in range(3):
         low, high = v_in[c, 0], v_in[c, 1]
         v_rows.append([low, high, delta0 * low, delta1 * high])
-        x_out[c * nz : (c + 1) * nz] = x0_parts[c] + dot(jnp.concatenate(v_rows[c], axis=1), val[...])
-
-    @pl.when(gy != 0)
-    def _():
-        tot_copy(0).wait_recv()
-
-    x_out[planes : planes + 8] = tot_in[...]
+    sent = [jnp.concatenate([v_rows[c][q] for c in range(3)], axis=0) for q in range(4)]
+    sent = jnp.concatenate(sent, axis=1)
+    high = sent.astype(jnp.bfloat16)
+    low = (sent - high.astype(F32)).astype(jnp.bfloat16)
+    pieces = jnp.dot(jnp.concatenate([high, low], axis=0), val[...], preferred_element_type=F32)
+    x_out[...] += pieces[:planes, :128] + (pieces[planes:, :128] + pieces[:planes, 128:])
+
 
     def x_copy(d):
         return pltpu.make_async_remote_copy(
@@ -418,10 +419,20 @@
         x_copy(d).start()
     x_in[gx] = x_out[...]
 
-    for c in range(3):
-        u_c = grad_o[c * nz * ny : (c + 1) * nz * ny, :] + dot(
-            sides[:, 8 * nz :], jnp.concatenate(v_rows[c], axis=0))
-        grad_o[c * nz * ny : (c + 1) * nz * ny, :] = dot(u_c, local[...])
+    @pl.when(gy != 0)
+    def _():
+        tot_copy(0).wait_recv()
+        for d in range(1, gx_n):
+            sum_copy(d).start()
+        sum_in[gx] = tot_in[...]
+
+    stores = []
+    for c in range(3):
+        part = pl.ds(c * nz * ny, nz * ny)
+        u_c = own[part, :] + dot(sides[:, 8 * nz :], jnp.concatenate(v_rows[c], axis=0))
+        own[part, :] = dot(u_c, local[...])
+        stores.append(pltpu.make_async_copy(own.at[part, :], grad_o.at[part, :], load_sem.at[c]))
+        stores[-1].start()
 
     pltpu.make_async_remote_copy(
         src_ref=x_in.at[0 : gx_n - 1], dst_ref=x_in.at[0 : gx_n - 1], send_sem=send_sem.at[11],
@@ -433,21 +444,24 @@
             value += mix[m, 0:1] * part
             to_r += mix[m, 1:2] * part
             to_p += mix[m, 2:3] * part
-        value += pltpu.roll(to_r, ny, 1) + pltpu.roll(to_p, 128 - ny, 1)
-        spread = jnp.broadcast_to(value[:, None, :], (nz, ny, 128)).reshape(nz * ny, 128)
-        spread = jnp.where(same_row, spread, 0.0)
-        grad_o[c * nz * ny : (c + 1) * nz * ny, :] += dot(spread, shapes[...])
-    total = x_in[0, planes : planes + 8]
+        small_o[c * nz : (c + 1) * nz] = value + pltpu.roll(to_r, ny, 1) + pltpu.roll(to_p, 128 - ny, 1)
+    pltpu.make_async_remote_copy(
+        src_ref=sum_in.at[0 : gx_n - 1], dst_ref=sum_in.at[0 : gx_n - 1], send_sem=send_sem.at[12],
+        recv_sem=recv_sem.at[7], device_id={"gx": 0}, device_id_type=MESH).wait_recv()
+    total = sum_in[0]
     for m in range(1, gx_n):
-        total = total + x_in[m, planes : planes + 8]
+        total = total + sum_in[m]
     mine = ((gx * gy_n + gy) * gz_n + gz).astype(F32)
     hit = (pltpu.roll(total, 4, 0) == mine) & (row < gy_n // 4) & (lane % 32 < gx_n * nx // PATCH)
-    act_o[...] = jnp.sum(jnp.where(hit, total, 0.0), keepdims=True)
-
-    for c in range(SOLVERS):
-        @pl.when(gy != c)
-        def _():
-            pq_copy(c).wait_send()
+    small_o[planes : planes + 8] = jnp.where(hit, total, 0.0)
+
+    for copy in stores:
+        copy.wait()
+
+    @pl.when(gy != 0)
+    def _():
+        pq_copy().wait_send()
+
     for side in (0, 1):
         halo_copy(side).wait_send()
 
@@ -460,49 +474,106 @@
         def _():
             wall_copy(0).wait_send()
 
-    @pl.when(gy < SOLVERS)
+    @pl.when(gy == 0)
     def _():
         pltpu.make_async_remote_copy(
-            src_ref=v_out.at[0 : gy_n - 1], dst_ref=v_out.at[0 : gy_n - 1], send_sem=send_sem.at[9],
-            recv_sem=v_sem.at[0], device_id={"gy": 0}, device_id_type=MESH).wait_send()
-
-    @pl.when(gy == 0)
-    def _():
+            src_ref=v_out.at[1:gy_n], dst_ref=v_out.at[1:gy_n], send_sem=send_sem.at[9],
+            recv_sem=recv_sem.at[6], device_id={"gy": 0}, device_id_type=MESH).wait_send()
         for k in range(1, gy_n):
             tot_copy(k).wait_send()
 
     for d in range(1, gx_n):
         x_copy(d).wait_send()
+        sum_copy(d).wait_send()
+
+
+def finish(sizes, part_h, small_h, shapes_h, grad_h, act_h, part, small, shapes, act, sem):
+    gx_n, gy_n, gz_n, ny, nx, nz = sizes
+    block = nz * ny
+    loads = [
+        pltpu.make_async_copy(small_h, small, sem.at[3]),
+        pltpu.make_async_copy(shapes_h.at[lax.axis_index("gx")], shapes, sem.at[4]),
+    ] + [
+        pltpu.make_async_copy(part_h.at[pl.ds(c * block, block), :], part.at[pl.ds(c * block, block), :], sem.at[c])
+        for c in range(3)
+    ]
+    for copy in loads:
+        copy.start()
+    same_row = (
+        lax.broadcasted_iota(jnp.int32, (block, 128), 0) % ny
+        == lax.broadcasted_iota(jnp.int32, (block, 128), 1) % ny
+    )
+    loads[0].wait()
+    loads[1].wait()
+    act[...] = jnp.sum(small[3 * nz :], keepdims=True)
+    stores = [pltpu.make_async_copy(act, act_h, sem.at[8])]
+    stores[0].start()
+    for c in range(3):
+        value = small[c * nz : (c + 1) * nz]
+        high = value.astype(jnp.bfloat16).astype(F32)
+        spread = [
+            jnp.where(same_row, jnp.broadcast_to(v[:, None, :], (nz, ny, 128)).reshape(block, 128), 0.0)
+            for v in (high, value - high)
+        ]
+        both = jnp.concatenate(spread, axis=1).astype(jnp.bfloat16)
+        added = jnp.dot(both, shapes[...], preferred_element_type=F32)
+        added = added[:, :nx] + added[:, nx:]
+        loads[2 + c].wait()
+        part[c * block : (c + 1) * block, :] += added
+        stores.append(
+            pltpu.make_async_copy(part.at[pl.ds(c * block, block), :], grad_h.at[pl.ds(c * block, block), :], sem.at[5 + c])
+        )
+        stores[-1].start()
+    for copy in stores:
+        copy.wait()
 
 
 def on_device(sizes, cst, cotangent, closure, owner, blowing):
     gx_n, gy_n, gz_n, ny, nx, nz = sizes
     f32 = lambda name: jnp.asarray(np.asarray(cst[name], np.float32))
-    tables = [f32(n) for n in ("inner", "pq", "sides", "fun", "val", "local", "shapes", "mix", "wall", "ends", "patch")]
+
+    def halves(name, axis):
+        exact = np.asarray(cst[name], np.float32)
+        high = exact.astype(jnp.bfloat16)
+        low = (exact - high.astype(np.float32)).astype(jnp.bfloat16)
+        return np.concatenate([high, low], axis=axis)
+
+    names = ("inner", "pq", "sides", "fun", "val", "local", "mix", "wall", "ends", "patch")
+    tables = [jnp.asarray(halves(n, 2)) if n == "val" else f32(n) for n in names]
     anyspec = pl.BlockSpec(memory_space=pltpu.HBM)
     vmem = pl.BlockSpec(memory_space=pltpu.VMEM)
     v = lambda *shape: pltpu.VMEM(shape, F32)
     rows = 3 * nz * ny
     scratch = [
         v(rows, nx), pltpu.VMEM((2, nz, nx), jnp.int32), pltpu.VMEM((ny, nx), jnp.int32), pltpu.SMEM((3,), F32),
-        v(nz * ny, nz * ny), v(2 * nz, nz * ny), v(nz * ny, 12 * nz), v(nx, 128), v(4 * nx, 128),
-        v(nx, nx), v(128, nx), v(gx_n, 4, 128), v(32, ny), v(2, 32, 128), v(nx, 128),
-        v(3, 2, nz, nx), v(gy_n, 2, nz, nx), v(2, 4, 3 * nz, nx), v(2, 4, 3 * nz, nx),
-        v(gy_n, 2, nz, nx), v(3, 2, nz, nx), v(8, 128), v(gy_n, 8, 128), v(8, 128), v(8, 128),
-        v(3 * nz + 8, 128), v(gx_n, 3 * nz + 8, 128),
-        pltpu.SemaphoreType.DMA((15,)), pltpu.SemaphoreType.DMA((12,)), pltpu.SemaphoreType.DMA((6,)),
-        pltpu.SemaphoreType.DMA((3,)),
+        v(nz * ny, nz * ny), v(2 * nz, nz * ny), v(nz * ny, 12 * nz), v(nx, 128), pltpu.VMEM((4 * nx, 256), jnp.bfloat16),
+        v(nx, nx), v(gx_n, 4, 128), v(32, ny), v(2, 32, 128), v(nx, 128),
+        v(3, 2, nz, nx), v(gy_n, 3, 2, nz, nx), v(2, 4, 3 * nz, nx), v(2, 4, 3 * nz, nx),
+        v(gy_n, 3, 2, nz, nx), v(3, 2, nz, nx), v(8, 128), v(gy_n, 8, 128), v(8, 128), v(8, 128),
+        v(3 * nz, 128), v(gx_n, 3 * nz, 128), v(gx_n, 8, 128), v(rows, nx),
+        pltpu.SemaphoreType.DMA((15,)), pltpu.SemaphoreType.DMA((13,)), pltpu.SemaphoreType.DMA((8,)),
     ]
-    gradient, share = pl.pallas_call(
+    part, small = pl.pallas_call(
         functools.partial(kernel, sizes, cst),
-        out_shape=(jax.ShapeDtypeStruct((rows, nx), F32), jax.ShapeDtypeStruct((1, 1), F32)),
+        out_shape=(jax.ShapeDtypeStruct((rows, nx), F32), jax.ShapeDtypeStruct((3 * nz + 8, 128), F32)),
         in_specs=[anyspec] * (4 + len(tables)),
-        out_specs=(vmem, vmem),
+        out_specs=(anyspec, vmem),
         scratch_shapes=scratch,
         compiler_params=pltpu.CompilerParams(
             collective_id=0, has_side_effects=True, vmem_limit_bytes=64 * 1024 * 1024
         ),
     )(cotangent.reshape(rows, nx), jnp.transpose(closure, (0, 2, 1)), owner.T, blowing, *tables)
+    shapes = jnp.asarray(np.tile(halves("shapes", 2), (1, 2, 1)))
+    gradient, share = pl.pallas_call(
+        functools.partial(finish, sizes),
+        out_shape=(jax.ShapeDtypeStruct((rows, nx), F32), jax.ShapeDtypeStruct((1, 1), F32)),
+        in_specs=[anyspec] * 3,
+        out_specs=(anyspec, anyspec),
+        scratch_shapes=[
+            v(rows, nx), v(3 * nz + 8, 128), pltpu.VMEM((256, 2 * nx), jnp.bfloat16), v(1, 1), pltpu.SemaphoreType.DMA((9,)),
+        ],
+        compiler_params=pltpu.CompilerParams(vmem_limit_bytes=64 * 1024 * 1024),
+    )(part, small, shapes)
     return gradient.reshape(cotangent.shape), share.reshape(1)
 
 

time: 34.6 us -> 32.4 us (0.936)
  local copies, waits for them, and re-layouts: 1.77 us -> 0 us
  between operations: 2.39 us -> 0.64 us
  Pallas kernels: 30.3 us -> 31.6 us
    pallas_call x0 -> x1, Pallas kernels: none -> 2.29 us  [on_device(): pl.pallas_call(functools.partial(finish, sizes), out_shape=(jax.ShapeDtyp...]
    unnamed x1 -> x0, local copies, waits for them, and re-layouts: 1.77 us -> none
    pallas_call x1, Pallas kernels: 30.3 us -> 29.3 us  [on_device(): pl.pallas_call(functools.partial(kernel, sizes, cst), out_shape=(jax.Shap...]
where the time goes in v2:
time: 32.4 us; the launch traced here: 32.2 us
  Pallas kernels  31.6 us (98%)
  between operations  0.64 us (2%)
    pallas_call x1, Pallas kernels, on_device(): pl.pallas_call(functools.partial(kernel, sizes, cst), out_shape=(jax.Shap...  29.3 us
    pallas_call x1, Pallas kernels, on_device(): pl.pallas_call(functools.partial(finish, sizes), out_shape=(jax.ShapeDtyp...  2.29 us

profile of v2, /device:TPU:1, one launch (start us, length us, event | category | flops | bytes accessed | tf_op | source)
XLA Modules:
  0.0 32.2 jit_solution(5789099599931146684)
XLA Ops:
  0.6 29.3 %shard_map.158 = (f32[768,128]{1,0:T(8,128)}, f32[32,128]{1,0:T(8,128)}) custom-call(f32[768,128]{1,0:T(8,128)} %bitcast.5, s32[2,8,128]{2,1,0:T(8,128)} %bitcast.7, s32[32,128]{1,0:T(8,128)} %bitcast.6, f32[3]{0:T(128)} %blow_h.1, f32[256,256]{1,0:T(8,128)} %constant.22.clone.inner_h, f32[16,256]{1,0:T(8,128)} %constant.23.clone.pq_h, ...), custom_call_target="tpu_custom_call" | custom-call | tf_op jit(solution)/shard_map/pallas_call | solution.py:556
  30.0 2.3 %shard_map.159 = (f32[768,128]{1,0:T(8,128)}, f32[1,1]{1,0:T(1,128)}) custom-call(f32[768,128]{1,0:T(8,128)} %get-tuple-element.6.part_h, f32[32,128]{1,0:T(8,128)} %get-tuple-element.7.small_h, bf16[8,256,256]{2,1,0:T(8,128)(2,1)} %constant.32.clone.shapes_h), custom_call_target="tpu_custom_call" | custom-call | tf_op jit(solution)/shard_map/pallas_call | solution.py:567
